TPU v7x, 32 devices: a whole 2x2x4 slice. The times are simulated.
32 devices in a mesh: src: 4 (over y, x), tgt: 8 (over z, core).
Axes of the slice: x: 2, y: 2, z: 4, core: 2. Of those that a mesh axis runs over, the one named last changes fastest.
Arguments:
- tile_cost: bfloat16 [384, 512, 512], P(('src', 'tgt')), may hold values from -2.5 to 7.5
- tile_pairs: int32 [384, 2], P(('src', 'tgt')), may hold values from 0 to 95, as said below
- tile_counts: int32 [32], P(('src', 'tgt')), may hold values from 3 to 12, as said below
- src_mass: float32 [12288], P('src'), may hold values from 0.25 to 4
- tgt_mass: float32 [49152], P('tgt'), may hold values from 0.25 to 4
- targets_t: bfloat16 [64, 49152], P(None, 'tgt'), may hold values from -18 to 18
Outputs:
- mapped_t: float32 [64, 12288], P(None, ('src', 'tgt'))
Inputs may be any that keep to these rules, and one draw needn't show every extreme that they name: `tile_pairs`: device d of the src+tgt order owns slots d * 12 to (d + 1) * 12 - 1. Its first tile_counts[d] slots hold distinct kept pairs whose source tile lies among its src index's 6 tiles and whose target tile among its tgt index's 12 tiles; its other slots repeat its first slot. Every source tile is in exactly 8 kept pairs, every target tile in at least one. `tile_counts`: over the devices of one src index the counts sum to 48; some device of every src index holds 12; every device holds at least (8 * 6 - 12) // (8 - 1) - 2.
All inputs are finite; a program needn't handle non-finite values.
Results may differ from a plain program's by a relative error of at most 0.0029.
Values may be sent and summed in bfloat16 or wider, within the bound.
A program may use at most 64 MiB of HBM per device.

v0:
```python
import jax
import jax.numpy as jnp
from jax import lax
from jax.sharding import PartitionSpec as P

ITERS = 2


entropic = 0.02
negative_floor = -1e30


def combined_all(array, axis, combine):
    everything = jax.tree.map(lambda part: lax.all_gather(part, axis), array)
    first = jax.tree.map(lambda part: part[0], everything)

    def hop(k, so_far):
        return combine(so_far, jax.tree.map(lambda part: part[k], everything))

    return lax.fori_loop(1, lax.axis_size(axis), hop, first)


def fold_pair(first, second):
    larger = jnp.maximum(first[0], second[0])
    return (larger, first[1] * jnp.exp(first[0] - larger) + second[1] * jnp.exp(second[0] - larger))


def merge_into(totals, position, part):
    before = (
        lax.dynamic_index_in_dim(totals[0], position, 0, False),
        lax.dynamic_index_in_dim(totals[1], position, 0, False),
    )
    after = fold_pair(before, part)
    return (
        lax.dynamic_update_index_in_dim(totals[0], after[0], position, 0),
        lax.dynamic_update_index_in_dim(totals[1], after[1], position, 0),
    )


def potential(merged, masses):
    return entropic * jnp.log(masses) - entropic * (merged[0] + jnp.log(merged[1])).reshape(-1)


def row_pass(costs, src_local, tgt_local, count, tgt_pot, totals):
    edge = costs.shape[1]

    def row_advance(slot_index, carry):
        cost_tile = costs[slot_index].astype(jnp.float32)
        column_pot = lax.dynamic_slice_in_dim(tgt_pot, tgt_local[slot_index] * edge, edge)
        scores = (column_pot[None, :] - cost_tile) / entropic
        maxima = jnp.max(scores, axis=1)
        sums = jnp.sum(jnp.exp(scores - maxima[:, None]), axis=1)
        return merge_into(carry, src_local[slot_index], (maxima, sums))

    return lax.fori_loop(0, count, row_advance, totals)


def col_pass(costs, src_local, tgt_local, count, src_pot, totals):
    edge = costs.shape[1]

    def col_advance(slot_index, carry):
        cost_tile = costs[slot_index].astype(jnp.float32)
        row_pot = lax.dynamic_slice_in_dim(src_pot, src_local[slot_index] * edge, edge)
        scores = (row_pot[:, None] - cost_tile) / entropic
        maxima = jnp.max(scores, axis=0)
        sums = jnp.sum(jnp.exp(scores - maxima[None, :]), axis=0)
        return merge_into(carry, tgt_local[slot_index], (maxima, sums))

    return lax.fori_loop(0, count, col_advance, totals)


def map_pass(costs, src_local, tgt_local, count, src_pot, tgt_pot, columns_all, totals):
    edge = costs.shape[1]

    def map_advance(slot_index, carry):
        numer, denom = carry
        src_tile = src_local[slot_index]
        tgt_tile = tgt_local[slot_index]
        cost_tile = costs[slot_index].astype(jnp.float32)
        row_pot = lax.dynamic_slice_in_dim(src_pot, src_tile * edge, edge)
        column_pot = lax.dynamic_slice_in_dim(tgt_pot, tgt_tile * edge, edge)
        weights = jnp.exp((row_pot[:, None] + column_pot[None, :] - cost_tile) / entropic)
        old_mass = lax.dynamic_index_in_dim(denom, src_tile, 0, False)
        denom = lax.dynamic_update_index_in_dim(
            denom, old_mass + jnp.sum(weights, axis=1), src_tile, 0
        )
        columns = lax.dynamic_slice_in_dim(columns_all, tgt_tile * edge, edge, 1)
        part = lax.dot_general(
            columns,
            weights.astype(jnp.bfloat16),
            (((1,), (1,)), ((), ())),
            preferred_element_type=jnp.float32,
        )
        current = lax.dynamic_slice_in_dim(numer, src_tile * edge, edge, 1)
        numer = lax.dynamic_update_slice_in_dim(numer, current + part, src_tile * edge, 1)
        return (numer, denom)

    return lax.fori_loop(0, count, map_advance, totals)


def local(tile_cost, tile_pairs, tile_counts, src_mass, tgt_mass, targets_t):
    edge = tile_cost.shape[1]
    src_tiles = src_mass.shape[0] // edge
    tgt_tiles = tgt_mass.shape[0] // edge
    src_local = tile_pairs[:, 0] % src_tiles
    tgt_local = tile_pairs[:, 1] % tgt_tiles
    own_count = tile_counts[0]
    row_empty = (
        jnp.full((src_tiles, edge), negative_floor, jnp.float32),
        jnp.zeros((src_tiles, edge), jnp.float32),
    )
    col_empty = (
        jnp.full((tgt_tiles, edge), negative_floor, jnp.float32),
        jnp.zeros((tgt_tiles, edge), jnp.float32),
    )
    tgt_pot = jnp.zeros(tgt_mass.shape, jnp.float32)
    src_pot = jnp.zeros(src_mass.shape, jnp.float32)
    for round_index in range(ITERS + 1):
        if round_index == ITERS:
            break
        row_parts = row_pass(tile_cost, src_local, tgt_local, own_count, tgt_pot, row_empty)
        src_pot = potential(combined_all(row_parts, "tgt", fold_pair), src_mass)
        col_parts = col_pass(tile_cost, src_local, tgt_local, own_count, src_pot, col_empty)
        tgt_pot = potential(combined_all(col_parts, "src", fold_pair), tgt_mass)
    start = (
        jnp.zeros((targets_t.shape[0], src_mass.shape[0]), jnp.float32),
        jnp.zeros((src_tiles, edge), jnp.float32),
    )
    totals = map_pass(
        tile_cost, src_local, tgt_local, own_count, src_pot, tgt_pot, targets_t, start
    )
    numer = totals[0]
    denom = totals[1].reshape(-1)
    numer, denom = lax.psum((numer, denom), "tgt")
    share = denom.shape[0] // lax.axis_size("tgt")
    offset = lax.axis_index("tgt") * share
    numer = lax.dynamic_slice_in_dim(numer, offset, share, 1)
    denom = lax.dynamic_slice_in_dim(denom, offset, share, 0)
    return numer / denom[None, :]


def solution(mesh):
    return jax.shard_map(
        local,
        mesh=mesh,
        in_specs=(
            P(("src", "tgt"), None, None),
            P(("src", "tgt"), None),
            P(("src", "tgt")),
            P("src"),
            P("tgt"),
            P(None, "tgt"),
        ),
        out_specs=P(None, ("src", "tgt")),
        check_vma=False,
    )
```

profile of v0, /device:TPU:0, one launch (start us, length us, event | category | flops | bytes accessed | tf_op | source)
XLA Modules:
  0.0 592.7 jit_solution(17301197210047742446)
XLA Ops:
  7.3 69.6 %while.128 = (s32[]{:T(128)}, f32[6,512]{1,0:T(8,128)S(1)}, f32[6,512]{1,0:T(8,128)S(1)}, s32[]{:T(128)}, s32[12]{0:T(128)S(1)}, /*index=5*/bf16[12,512,512]{2,1...) while((s32[]{:T(128)}, f32[6,512]{1,0:T(8,128)S(1)}, f32[6,512]{1,0:T(8,128)S(1)}, s32[]{:T(128)}, ...), condition=%wide.region_3.4_spmd, body=%wide.region_0.3_spmd.sunk | while | flops 2361352 | bytes 1075401 | solution.py:55
  77.0 14.0 %all-gather.9 = f32[8,6,512]{2,1,0:T(8,128)S(1)} all-gather(f32[1,6,512]{2,1,0:T(8,128)S(1)} %bitcast.195), channel_id=3, replica_groups=mesh['src'=4,'tgt'=8] {'tgt'}, dimensions={0}, use_global_device_ids=true | all-gather | bytes 110592 | tf_op jit(solution)/shard_map/all_gather | solution.py:14
  90.9 14.0 %all-gather.8 = f32[8,6,512]{2,1,0:T(8,128)S(1)} all-gather(f32[1,6,512]{2,1,0:T(8,128)S(1)} %bitcast.196), channel_id=2, replica_groups=mesh['src'=4,'tgt'=8] {'tgt'}, dimensions={0}, use_global_device_ids=true | all-gather | bytes 110592 | tf_op jit(solution)/shard_map/all_gather | solution.py:14
  105.3 84.2 %while.130 = (s32[]{:T(128)}, f32[12,512]{1,0:T(8,128)S(1)}, f32[12,512]{1,0:T(8,128)S(1)}, s32[]{:T(128)}, s32[12]{0:T(128)S(1)}, /*index=5*/s32[12]{0:T(128)S(...) while((s32[]{:T(128)}, f32[12,512]{1,0:T(8,128)S(1)}, ...), condition=%wide.region_9.10_spmd, body=%wide.region_6.9_spmd.sunk | while | flops 2361356 | bytes 1083679 | solution.py:69
  189.5 6.9 %all-gather.11 = f32[4,12,512]{2,1,0:T(8,128)S(1)} all-gather(f32[1,12,512]{2,1,0:T(8,128)S(1)} %bitcast.193), channel_id=5, replica_groups=mesh['src'=4,'tgt'=8] {'src'}, dimensions={0}, use_global_device_ids=true | all-gather | bytes 122880 | tf_op jit(solution)/shard_map/all_gather | solution.py:14
  196.5 9.0 %all-gather.10 = f32[4,12,512]{2,1,0:T(8,128)S(1)} all-gather(f32[1,12,512]{2,1,0:T(8,128)S(1)} %bitcast.192), channel_id=4, replica_groups=mesh['src'=4,'tgt'=8] {'src'}, dimensions={0}, use_global_device_ids=true | all-gather | bytes 122880 | tf_op jit(solution)/shard_map/all_gather | solution.py:14
  205.8 87.5 %while.132 = (s32[]{:T(128)}, f32[6,512]{1,0:T(8,128)S(1)}, f32[6,512]{1,0:T(8,128)S(1)}, s32[]{:T(128)}, s32[12]{0:T(128)S(1)}, /*index=5*/s32[12]{0:T(128)S(1)...) while((s32[]{:T(128)}, f32[6,512]{1,0:T(8,128)S(1)}, ...), condition=%wide.region_15.16_spmd, body=%wide.region_12.15_spmd.sunk | while | flops 2361356 | bytes 1083687 | solution.py:55
  293.3 14.0 %all-gather.13 = f32[8,6,512]{2,1,0:T(8,128)S(1)} all-gather(f32[1,6,512]{2,1,0:T(8,128)S(1)} %bitcast.197), channel_id=7, replica_groups=mesh['src'=4,'tgt'=8] {'tgt'}, dimensions={0}, use_global_device_ids=true | all-gather | bytes 110592 | tf_op jit(solution)/shard_map/all_gather | solution.py:14
  307.3 14.0 %all-gather.12 = f32[8,6,512]{2,1,0:T(8,128)S(1)} all-gather(f32[1,6,512]{2,1,0:T(8,128)S(1)} %bitcast.198), channel_id=6, replica_groups=mesh['src'=4,'tgt'=8] {'tgt'}, dimensions={0}, use_global_device_ids=true | all-gather | bytes 110592 | tf_op jit(solution)/shard_map/all_gather | solution.py:14
  321.6 88.6 %while.134 = (s32[]{:T(128)}, f32[12,512]{1,0:T(8,128)S(1)}, f32[12,512]{1,0:T(8,128)S(1)}, s32[]{:T(128)}, s32[12]{0:T(128)S(1)}, /*index=5*/s32[12]{0:T(128)S(...) while((s32[]{:T(128)}, f32[12,512]{1,0:T(8,128)S(1)}, ...), condition=%wide.region_21.22_spmd, body=%wide.region_18.21_spmd.sunk | while | flops 2361356 | bytes 1083679 | solution.py:69
  410.3 6.9 %all-gather.15 = f32[4,12,512]{2,1,0:T(8,128)S(1)} all-gather(f32[1,12,512]{2,1,0:T(8,128)S(1)} %bitcast.194), channel_id=9, replica_groups=mesh['src'=4,'tgt'=8] {'src'}, dimensions={0}, use_global_device_ids=true | all-gather | bytes 122880 | tf_op jit(solution)/shard_map/all_gather | solution.py:14
  417.2 9.0 %all-gather.14 = f32[4,12,512]{2,1,0:T(8,128)S(1)} all-gather(f32[1,12,512]{2,1,0:T(8,128)S(1)} %bitcast.191), channel_id=8, replica_groups=mesh['src'=4,'tgt'=8] {'src'}, dimensions={0}, use_global_device_ids=true | all-gather | bytes 122880 | tf_op jit(solution)/shard_map/all_gather | solution.py:14
  426.5 103.0 %while.136 = (s32[]{:T(128)}, f32[64,3072]{1,0:T(8,128)S(1)}, f32[6,512]{1,0:T(8,128)S(1)}, s32[]{:T(128)}, s32[12]{0:T(128)S(1)}, /*index=5*/s32[12]{0:T(128)S(...) while((s32[]{:T(128)}, f32[64,3072]{1,0:T(8,128)S(1)}, ...), condition=%wide.region_26.27_spmd, body=%wide.region_24.26_spmd.sunk | while | flops 36208652 | bytes 1405309 | solution.py:98
  429.9 1.6 fusion.74
  438.4 1.6 fusion.74
  446.9 1.6 fusion.74
  455.5 1.6 fusion.74
  457.0 1.4 fusion.75
  464.0 1.6 fusion.74
  465.6 1.4 fusion.75
  472.5 1.6 fusion.74
  481.1 1.6 fusion.74
  489.6 1.6 fusion.74
  498.1 1.6 fusion.74
  499.7 1.4 fusion.75
  506.7 1.6 fusion.74
  508.2 1.4 fusion.75
  515.2 1.6 fusion.74
  523.7 1.6 fusion.74
  530.5 26.4 %psum.15 = f32[3072]{0:T(1024)S(1)} all-reduce(f32[3072]{0:T(1024)S(1)} %reshape.63), channel_id=1, replica_groups=mesh['src'=4,'tgt'=8] {'tgt'}, use_global_device_ids=true, to_apply=%region_28.29 | all-reduce | flops 3072 | bytes 24576 | tf_op jit(solution)/shard_map/psum | solution.py:134
  557.0 27.4 %all-reduce.2.cloned.1.call-done = f32[64,3072]{1,0:T(8,128)} async-done(((f32[64,3072]{1,0:T(8,128)}), f32[64,3072]{1,0:T(8,128)}) %all-reduce.2.cloned.1.call-update) | async-done | bytes 786448 | tf_op jit(solution)/shard_map/psum | solution.py:134
  584.3 1.5 dynamic-slice_divide_fusion
  (505 shorter events, 219.6 us)
Async XLA Ops:
  6.5 98.7 %copy-start.2 = (f32[3072]{0:T(1024)S(1)}, f32[3072]{0:T(1024)}, u32[]{:S(2)}) copy-start(f32[3072]{0:T(1024)} %param.27) | copy-start | bytes 36868
  6.5 577.8 %all-reduce.2.cloned.1.call-start = ((), (), s32[]{:S(2)}) async-start(), calls=%async_computation | async-start | bytes 1572864 | tf_op jit(solution)/shard_map/psum | solution.py:134
  7.3 198.4 %copy-start.1 = (f32[6144]{0:T(1024)S(1)}, f32[6144]{0:T(1024)}, u32[]{:S(2)}) copy-start(f32[6144]{0:T(1024)} %param.28) | copy-start | bytes 73732
  529.6 0.9 copy-start
Sparse Core Ops, SparseCore 0:
  530.6 53.6 all-reduce.1
where the time goes:
time: 602 us; the launch traced here: 593 us
  loops' own time  193 us (32%)
  other arithmetic  148 us (25%)
  blocking collectives  114 us (19%)
  local copies, waits for them, and re-layouts  77.9 us (13%)
  waiting for transfers between devices  27.4 us (5%)
  matrix products  19 us (3%)
  between operations  13.7 us (2%)
    all_gather x8, blocking collectives, combined_all(): everything = jax.tree.map(lambda part: lax.all_gather(part, axis), array)  87.7 us
    another operation x2, loops' own time, col_pass(): return lax.fori_loop(0, count, col_advance, totals)  75.7 us
    another operation x2, loops' own time, row_pass(): return lax.fori_loop(0, count, row_advance, totals)  67.4 us
    another operation x1, loops' own time, map_pass(): return lax.fori_loop(0, count, map_advance, totals)  49 us
    reduce_sum x24, other arithmetic, row_advance(): sums = jnp.sum(jnp.exp(scores - maxima[:, None]), axis=1)  33.4 us
    reduce_sum x24, other arithmetic, col_advance(): sums = jnp.sum(jnp.exp(scores - maxima[None, :]), axis=0)  32.8 us
    reduce_max x24, other arithmetic, col_advance(): maxima = jnp.max(scores, axis=0)  30.1 us
    reduce_max x24, other arithmetic, row_advance(): maxima = jnp.max(scores, axis=1)  30.1 us
  transfers between devices with their start and end apart: 1, of which 1 were waited for; matrix products, arithmetic and copies ran while one was open for 0% of the time, Pallas kernels for 0%

commit v1 on v0

v1 whole, which is shorter than its diff:
```python
import functools

import jax
import jax.numpy as jnp
from jax import lax
from jax.experimental import pallas as pl
from jax.experimental.pallas import tpu as pltpu
from jax.sharding import PartitionSpec as P

MESH = pl.DeviceIdType.MESH
inverse_eps = 50.0
negative_floor = -1e30
ROWS = 64
LANES = 128
PAD = 16


def logsumexp0(parts):
    top = jnp.max(parts, axis=0)
    return top + jnp.log(jnp.sum(jnp.exp(parts - top[None]), axis=0))


def kernel(
    n_src,
    n_tgt,
    pairs_ref,
    count_ref,
    cost_hbm,
    src_mass_ref,
    tgt_mass_ref,
    targets_hbm,
    out_ref,
    cost,
    q,
    tgts,
    prods,
    slot_cols,
    slot_rows,
    pad_rows,
    row_pot,
    col_stab,
    col_sum,
    col_fac,
    tgt_pot,
    row_buf1,
    row_buf2,
    col_buf1,
    col_buf2,
    out_send,
    out_recv,
    cost_sem,
    tgts_sem,
    row_send1,
    row_recv1,
    row_send2,
    row_recv2,
    col_send1,
    col_recv1,
    col_send2,
    col_recv2,
    out_send_sem,
    out_recv_sem,
):
    cap, edge = cost.shape[0], cost.shape[1]
    src_tiles, tgt_tiles = src_mass_ref.shape[0], tgt_mass_ref.shape[0]
    dim = targets_hbm.shape[0]
    my_src, my_tgt = lax.axis_index("src"), lax.axis_index("tgt")
    chunks = edge // ROWS

    for k in range(cap):
        pltpu.make_async_copy(cost_hbm.at[k], cost.at[k], cost_sem.at[k]).start()
    for t in range(tgt_tiles):
        pltpu.make_async_copy(
            targets_hbm.at[:, pl.ds(t * edge, edge)], tgts.at[t, pl.ds(0, dim)], tgts_sem.at[t]
        ).start()

    barrier = pltpu.get_barrier_semaphore()
    for off in range(1, n_tgt):
        pl.semaphore_signal(
            barrier, inc=1, device_id={"tgt": lax.rem(my_tgt + off, n_tgt)}, device_id_type=MESH
        )
    for off in range(1, n_src):
        pl.semaphore_signal(
            barrier, inc=1, device_id={"src": lax.rem(my_src + off, n_src)}, device_id_type=MESH
        )

    pad_rows[...] = jnp.zeros_like(pad_rows)
    slot_cols[...] = jnp.zeros_like(slot_cols)
    tgts[:, dim:, :] = jnp.ones((tgt_tiles, PAD, edge), jnp.bfloat16)

    count = count_ref[0]
    src_of = [lax.rem(pairs_ref[k, 0], src_tiles) for k in range(cap)]
    tgt_of = [lax.rem(pairs_ref[k, 1], tgt_tiles) for k in range(cap)]
    src_id = [jnp.where(k < count, src_of[k], -1) for k in range(cap)]
    tgt_id = [jnp.where(k < count, tgt_of[k], -1) for k in range(cap)]
    src_rows = lax.broadcasted_iota(jnp.int32, (src_tiles, edge), 0)
    tgt_rows = lax.broadcasted_iota(jnp.int32, (tgt_tiles, edge), 0)
    lane = lax.broadcasted_iota(jnp.int32, (ROWS, LANES), 1)

    def wide(block):
        return jnp.concatenate([block] * (edge // LANES), axis=1)

    def put_column(k, c, value):
        rows = slice(c * ROWS, (c + 1) * ROWS)
        slot_cols[rows, :] = jnp.where(lane == k, value, slot_cols[rows, :])

    def slots_as_rows():
        slot_rows[...] = slot_cols[...].T[:PAD]

    def spread_rows(values):
        pad_rows[0:src_tiles, :] = values
        columns = pad_rows[...].T
        for s in range(src_tiles):
            row_pot[s] = jnp.broadcast_to(columns[:, s : s + 1], (edge, LANES))

    def exchange(buf, axis, me, n, send_sem, recv_sem):
        copies = []
        for off in range(1, n):
            copy = pltpu.make_async_remote_copy(
                src_ref=buf.at[0],
                dst_ref=buf.at[off],
                send_sem=send_sem.at[off - 1],
                recv_sem=recv_sem.at[off - 1],
                device_id={axis: lax.rem(me + off, n)},
                device_id_type=MESH,
            )
            copy.start()
            copies.append(copy)
        for copy in copies:
            copy.wait()

    def merge_logs(parts, ids, rows):
        top = jnp.full(rows.shape, negative_floor, jnp.float32)
        for part, tile in zip(parts, ids):
            top = jnp.maximum(top, jnp.where(rows == tile, part, negative_floor))
        total = jnp.zeros(rows.shape, jnp.float32)
        for part, tile in zip(parts, ids):
            total = total + jnp.where(rows == tile, jnp.exp(part - top), 0.0)
        return jnp.where(total > 0.0, top + jnp.log(total), negative_floor)

    def merge_sums(parts, ids, rows):
        total = jnp.zeros(rows.shape, jnp.float32)
        for part, tile in zip(parts, ids):
            total = total + jnp.where(rows == tile, part, 0.0)
        return total

    def row_first(k, carry):
        pltpu.make_async_copy(cost_hbm.at[k], cost.at[k], cost_sem.at[k]).wait()
        for c in range(chunks):
            tile = cost[k, c * ROWS : (c + 1) * ROWS, :].astype(jnp.float32)
            low = jnp.min(tile, axis=1, keepdims=True)
            total = jnp.sum(jnp.exp((low - tile) * inverse_eps), axis=1, keepdims=True)
            put_column(k, c, jnp.log(total) - low * inverse_eps)
        return carry

    lax.fori_loop(0, cap, row_first, 0)
    slots_as_rows()
    row_buf1[0] = merge_logs([slot_rows[k : k + 1, :] for k in range(cap)], src_id, src_rows)
    pl.semaphore_wait(barrier, n_tgt - 1 + n_src - 1)
    exchange(row_buf1, "tgt", my_tgt, n_tgt, row_send1, row_recv1)
    spread_rows(jnp.log(src_mass_ref[...]) - logsumexp0(row_buf1[...]))

    def col_first(k, carry):
        s = lax.rem(pairs_ref[k, 0], src_tiles)
        top = jnp.full((8, edge), negative_floor, jnp.float32)
        for c in range(chunks):
            rows = slice(c * ROWS, (c + 1) * ROWS)
            score = wide(row_pot[s, rows, :]) - cost[k, rows, :].astype(jnp.float32) * inverse_eps
            q[k, rows, :] = score
            top = jnp.maximum(top, jnp.max(score.reshape(ROWS // 8, 8, edge), axis=0))
        top = jnp.broadcast_to(jnp.max(top, axis=0, keepdims=True), (8, edge))
        total = jnp.zeros((8, edge), jnp.float32)
        for c in range(chunks):
            rows = slice(c * ROWS, (c + 1) * ROWS)
            value = jnp.exp(q[k, rows, :].reshape(ROWS // 8, 8, edge) - top[None])
            q[k, rows, :] = value.reshape(ROWS, edge)
            total = total + jnp.sum(value, axis=0)
        col_stab[k] = top
        col_sum[k] = jnp.broadcast_to(jnp.sum(total, axis=0, keepdims=True), (8, edge))
        return carry

    lax.fori_loop(0, cap, col_first, 0)
    col_buf1[0] = merge_logs(
        [col_stab[k, 0:1, :] + jnp.log(col_sum[k, 0:1, :]) for k in range(cap)], tgt_id, tgt_rows
    )
    exchange(col_buf1, "src", my_src, n_src, col_send1, col_recv1)
    potential = jnp.log(tgt_mass_ref[...]) - logsumexp0(col_buf1[...])
    for t in range(tgt_tiles):
        tgt_pot[t] = jnp.broadcast_to(potential[t : t + 1, :], (8, edge))

    def row_second(k, carry):
        t = lax.rem(pairs_ref[k, 1], tgt_tiles)
        alive = jnp.full((8, edge), k, jnp.int32) < count
        factor = jnp.where(alive, jnp.exp(tgt_pot[t] + col_stab[k]), 0.0)
        col_fac[k] = factor
        for c in range(chunks):
            rows = slice(c * ROWS, (c + 1) * ROWS)
            value = q[k, rows, :].reshape(ROWS // 8, 8, edge) * factor[None]
            put_column(k, c, jnp.sum(value.reshape(ROWS, edge), axis=1, keepdims=True))
        return carry

    lax.fori_loop(0, cap, row_second, 0)
    slots_as_rows()
    row_buf2[0] = merge_sums([slot_rows[k : k + 1, :] for k in range(cap)], src_id, src_rows)
    exchange(row_buf2, "tgt", my_tgt, n_tgt, row_send2, row_recv2)
    spread_rows(src_mass_ref[...] / jnp.sum(row_buf2[...], axis=0))

    def col_second(k, carry):
        s = lax.rem(pairs_ref[k, 0], src_tiles)
        total = jnp.zeros((8, edge), jnp.float32)
        for c in range(chunks):
            rows = slice(c * ROWS, (c + 1) * ROWS)
            value = q[k, rows, :] * wide(row_pot[s, rows, :])
            total = total + jnp.sum(value.reshape(ROWS // 8, 8, edge), axis=0)
        col_sum[k] = jnp.broadcast_to(jnp.sum(total, axis=0, keepdims=True), (8, edge)) * col_fac[k]
        return carry

    lax.fori_loop(0, cap, col_second, 0)
    col_buf2[0] = merge_sums([col_sum[k, 0:1, :] for k in range(cap)], tgt_id, tgt_rows)
    exchange(col_buf2, "src", my_src, n_src, col_send2, col_recv2)
    potential = tgt_mass_ref[...] / jnp.sum(col_buf2[...], axis=0)
    for t in range(tgt_tiles):
        tgt_pot[t] = jnp.broadcast_to(potential[t : t + 1, :], (8, edge))

    for t in range(tgt_tiles):
        pltpu.make_async_copy(
            targets_hbm.at[:, pl.ds(t * edge, edge)], tgts.at[t, pl.ds(0, dim)], tgts_sem.at[t]
        ).wait()

    def map_slot(k, carry):
        s = lax.rem(pairs_ref[k, 0], src_tiles)
        t = lax.rem(pairs_ref[k, 1], tgt_tiles)
        factor = tgt_pot[t] * col_fac[k]
        left = tgts[t]
        for h in range(edge // 256):
            parts = []
            for c in range(256 // ROWS):
                rows = slice(h * 256 + c * ROWS, h * 256 + (c + 1) * ROWS)
                value = (q[k, rows, :] * wide(row_pot[s, rows, :])).reshape(ROWS // 8, 8, edge)
                parts.append((value * factor[None]).reshape(ROWS, edge).astype(jnp.bfloat16))
            prods[k, :, h * 256 : (h + 1) * 256] = lax.dot_general(
                left,
                jnp.concatenate(parts, axis=0),
                (((1,), (1,)), ((), ())),
                preferred_element_type=jnp.float32,
            )
        return carry

    lax.fori_loop(0, cap, map_slot, 0)

    share = out_ref.shape[1]
    tall = dim + PAD
    low_half = lax.broadcasted_iota(jnp.int32, (tall, LANES), 0) >= dim + PAD // 2
    for s in range(src_tiles):
        picks = [jnp.where(src_id[k] == s, 1.0, 0.0) for k in range(cap)]
        for c in range(edge // LANES):
            total = jnp.zeros((tall, LANES), jnp.float32)
            for k in range(cap):
                total = total + prods[k, :, c * LANES : (c + 1) * LANES] * picks[k]
            rest = total - total.astype(jnp.bfloat16).astype(jnp.float32)
            total = jnp.where(low_half, rest, total)
            place = s * edge + c * LANES
            start = place % share
            out_send[place // share, :, start : start + LANES] = total.astype(jnp.bfloat16)

    copies = []
    for off in range(1, n_tgt):
        peer = lax.rem(my_tgt + off, n_tgt)
        copy = pltpu.make_async_remote_copy(
            src_ref=out_send.at[peer],
            dst_ref=out_recv.at[off - 1],
            send_sem=out_send_sem.at[off - 1],
            recv_sem=out_recv_sem.at[off - 1],
            device_id={"tgt": peer},
            device_id_type=MESH,
        )
        copy.start()
        copies.append(copy)
    total = out_send[my_tgt].astype(jnp.float32)
    for off, copy in enumerate(copies):
        copy.wait()
        total = total + out_recv[off].astype(jnp.float32)
    mass = total[dim : dim + 1] + total[dim + PAD // 2 : dim + PAD // 2 + 1]
    out_ref[...] = total[:dim] / mass


def local(n_src, n_tgt, tile_cost, tile_pairs, tile_counts, src_mass, tgt_mass, targets_t):
    cap, edge = tile_cost.shape[0], tile_cost.shape[1]
    src_tiles, tgt_tiles = src_mass.shape[0] // edge, tgt_mass.shape[0] // edge
    dim = targets_t.shape[0]
    share = src_mass.shape[0] // n_tgt
    tall = dim + PAD
    f32, bf16 = jnp.float32, jnp.bfloat16
    dma = pltpu.SemaphoreType.DMA
    smem = pl.BlockSpec(memory_space=pltpu.SMEM)
    vmem = pl.BlockSpec(memory_space=pltpu.VMEM)
    hbm = pl.BlockSpec(memory_space=pl.ANY)
    return pl.pallas_call(
        functools.partial(kernel, n_src, n_tgt),
        out_shape=jax.ShapeDtypeStruct((dim, share), f32),
        in_specs=[smem, smem, hbm, vmem, vmem, hbm],
        out_specs=vmem,
        scratch_shapes=[
            pltpu.VMEM((cap, edge, edge), bf16),
            pltpu.VMEM((cap, edge, edge), f32),
            pltpu.VMEM((tgt_tiles, tall, edge), bf16),
            pltpu.VMEM((cap, tall, edge), f32),
            pltpu.VMEM((edge, LANES), f32),
            pltpu.VMEM((PAD, edge), f32),
            pltpu.VMEM((LANES, edge), f32),
            pltpu.VMEM((src_tiles, edge, LANES), f32),
            pltpu.VMEM((cap, 8, edge), f32),
            pltpu.VMEM((cap, 8, edge), f32),
            pltpu.VMEM((cap, 8, edge), f32),
            pltpu.VMEM((tgt_tiles, 8, edge), f32),
            pltpu.VMEM((n_tgt, src_tiles, edge), f32),
            pltpu.VMEM((n_tgt, src_tiles, edge), f32),
            pltpu.VMEM((n_src, tgt_tiles, edge), f32),
            pltpu.VMEM((n_src, tgt_tiles, edge), f32),
            pltpu.VMEM((n_tgt, tall, share), bf16),
            pltpu.VMEM((n_tgt - 1, tall, share), bf16),
            dma((cap,)),
            dma((tgt_tiles,)),
            dma((n_tgt - 1,)),
            dma((n_tgt - 1,)),
            dma((n_tgt - 1,)),
            dma((n_tgt - 1,)),
            dma((n_src - 1,)),
            dma((n_src - 1,)),
            dma((n_src - 1,)),
            dma((n_src - 1,)),
            dma((n_tgt - 1,)),
            dma((n_tgt - 1,)),
        ],
        compiler_params=pltpu.CompilerParams(
            collective_id=0, has_side_effects=True, vmem_limit_bytes=56 * 1024 * 1024
        ),
    )(
        tile_pairs,
        tile_counts,
        tile_cost,
        src_mass.reshape(src_tiles, edge),
        tgt_mass.reshape(tgt_tiles, edge),
        targets_t,
    )


def solution(mesh):
    return jax.shard_map(
        functools.partial(local, mesh.shape["src"], mesh.shape["tgt"]),
        mesh=mesh,
        in_specs=(
            P(("src", "tgt"), None, None),
            P(("src", "tgt"), None),
            P(("src", "tgt")),
            P("src"),
            P("tgt"),
            P(None, "tgt"),
        ),
        out_specs=P(None, ("src", "tgt")),
        check_vma=False,
    )
```

time: 602 us -> 56.3 us (0.09); the launches traced: 593 us -> 55.3 us
  loops' own time: 193 us -> 0 us
  other arithmetic: 148 us -> 0 us
  blocking collectives: 114 us -> 0 us
  local copies, waits for them, and re-layouts: 77.9 us -> 5.56 us
  Pallas kernels: 0 us -> 49 us
  waiting for transfers between devices: 27.4 us -> 0 us
  matrix products: 19 us -> 0 us
  between operations: 13.7 us -> 0.66 us
    another operation x9 -> x0, loops' own time: 193 us -> none  [the longest x2 75.7 us: col_pass(): return lax.fori_loop(0, count, col_advance, totals)]
    all_gather x8 -> x0, blocking collectives: 87.7 us -> none  [combined_all(): everything = jax.tree.map(lambda part: lax.all_gather(part, axis), array)]
    reduce_sum x60 -> x0, other arithmetic: 83.6 us -> none  [the longest x24 33.4 us: row_advance(): sums = jnp.sum(jnp.exp(scores - maxima[:, None]), axis=1)]
    dynamic_slice x169 -> x0, local copies, waits for them, and re-layouts: 70.1 us -> none  [the longest x24 14.4 us: row_advance(): return merge_into(carry, src_local[slot_index], (maxima, sums))]
    reduce_max x48 -> x0, other arithmetic: 60.2 us -> none  [the longest x24 30.1 us: col_advance(): maxima = jnp.max(scores, axis=0)]
    pallas_call x0 -> x1, Pallas kernels: none -> 49 us  [local(): pl.pallas_call(functools.partial(kernel, n_src, n_tgt), out_shape=jax.Sha...]
    psum x1 -> x0, waiting for transfers between devices: 27.4 us -> none  [local(): numer, denom = lax.psum((numer, denom), 'tgt')]
    psum x1 -> x0, blocking collectives: 26.4 us -> none  [local(): numer, denom = lax.psum((numer, denom), 'tgt')]
  transfers between devices with their start and end apart: 1 -> 0, of which waited for: 1 -> 0; matrix products, arithmetic and copies ran while one was open for 0% -> 0% of each run, Pallas kernels for 0% -> 0%
where the time goes in v1:
time: 56.3 us; the launch traced here: 55.3 us
  Pallas kernels  49 us (87%)
  local copies, waits for them, and re-layouts  5.56 us (10%)
  between operations  0.66 us (1%)
    pallas_call x1, Pallas kernels, local(): pl.pallas_call(functools.partial(kernel, n_src, n_tgt), out_shape=jax.Sha...  49 us
    unnamed x2, local copies, waits for them, and re-layouts  2.9 us
    reshape x1, local copies, waits for them, and re-layouts, local(): tgt_mass.reshape(tgt_tiles, edge)  1.35 us
    reshape x1, local copies, waits for them, and re-layouts, local(): src_mass.reshape(src_tiles, edge)  1.31 us

profile of v1, /device:TPU:0, one launch (start us, length us, event | category | flops | bytes accessed | tf_op | source)
XLA Modules:
  0.0 55.3 jit_solution(4095017812920343090)
XLA Ops:
  0.7 1.4 %copy.7.pairs_ref = s32[12,2]{1,0:T(8,128)} copy(s32[12,2]{0,1:T(2,128)} %param.7) | data formatting | bytes 192 | tf_op args[1]
  2.0 1.3 %reshape.6.src_mass_ref = f32[6,512]{1,0:T(8,128)} reshape(f32[3072]{0:T(1024)} %param.9) | data formatting | bytes 24576 | tf_op jit(solution)/shard_map/reshape | solution.py:342
  3.3 1.4 %reshape.7.tgt_mass_ref = f32[12,512]{1,0:T(8,128)} reshape(f32[6144]{0:T(1024)} %param.10) | data formatting | bytes 49152 | tf_op jit(solution)/shard_map/reshape | solution.py:343
  4.7 49.0 %shard_map.64 = f32[64,384]{1,0:T(8,128)} custom-call(s32[12,2]{1,0:T(8,128)} %copy.7.pairs_ref, s32[1]{0:T(128)S(6)} %copy.9.count_ref, bf16[12,512,512]{2,1,0:T(8,128)(2,1)} %cost_hbm.1, f32[6,512]{1,0:T(8,128)} %reshape.6.src_mass_ref, f32[12,512]{1,0:T(8,128)} %reshape.7.tgt_mass_ref, bf16[64,6144]{1,0:T(8,128)(2,1)} %targets_hbm.1), custom_call_target="tpu_custom_call" | custom-call | tf_op jit(solution)/shard_map/pallas_call | solution.py:298
  53.7 1.5 %copy.10 = f32[64,384]{1,0:T(8,128)} copy(f32[64,384]{1,0:T(8,128)} %shard_map.64) | data formatting | bytes 196608

commit v2 on v1

--- a/solution.py
+++ b/solution.py
@@ -8,7 +8,7 @@
 from jax.sharding import PartitionSpec as P
 
 MESH = pl.DeviceIdType.MESH
-inverse_eps = 50.0
+inverse_eps = 50.0 * 1.4426950408889634
 negative_floor = -1e30
 ROWS = 64
 LANES = 128
@@ -17,7 +17,7 @@
 
 def logsumexp0(parts):
     top = jnp.max(parts, axis=0)
-    return top + jnp.log(jnp.sum(jnp.exp(parts - top[None]), axis=0))
+    return top + jnp.log2(jnp.sum(jnp.exp2(parts - top[None]), axis=0))
 
 
 def kernel(
@@ -26,8 +26,8 @@
     pairs_ref,
     count_ref,
     cost_hbm,
-    src_mass_ref,
-    tgt_mass_ref,
+    src_mass_flat,
+    tgt_mass_flat,
     targets_hbm,
     out_ref,
     cost,
@@ -42,10 +42,14 @@
     col_sum,
     col_fac,
     tgt_pot,
+    src_mass_ref,
+    tgt_mass_ref,
     row_buf1,
     row_buf2,
     col_buf1,
     col_buf2,
+    out_part,
+    pair_recv,
     out_send,
     out_recv,
     cost_sem,
@@ -58,6 +62,8 @@
     col_recv1,
     col_send2,
     col_recv2,
+    pair_send_sem,
+    pair_recv_sem,
     out_send_sem,
     out_recv_sem,
 ):
@@ -88,9 +94,14 @@
     slot_cols[...] = jnp.zeros_like(slot_cols)
     tgts[:, dim:, :] = jnp.ones((tgt_tiles, PAD, edge), jnp.bfloat16)
 
+    for s in range(src_tiles):
+        src_mass_ref[s : s + 1, :] = src_mass_flat[s * edge : (s + 1) * edge].reshape(1, edge)
+    for t in range(tgt_tiles):
+        tgt_mass_ref[t : t + 1, :] = tgt_mass_flat[t * edge : (t + 1) * edge].reshape(1, edge)
+
     count = count_ref[0]
-    src_of = [lax.rem(pairs_ref[k, 0], src_tiles) for k in range(cap)]
-    tgt_of = [lax.rem(pairs_ref[k, 1], tgt_tiles) for k in range(cap)]
+    src_of = [lax.rem(pairs_ref[0, k], src_tiles) for k in range(cap)]
+    tgt_of = [lax.rem(pairs_ref[1, k], tgt_tiles) for k in range(cap)]
     src_id = [jnp.where(k < count, src_of[k], -1) for k in range(cap)]
     tgt_id = [jnp.where(k < count, tgt_of[k], -1) for k in range(cap)]
     src_rows = lax.broadcasted_iota(jnp.int32, (src_tiles, edge), 0)
@@ -135,8 +146,8 @@
             top = jnp.maximum(top, jnp.where(rows == tile, part, negative_floor))
         total = jnp.zeros(rows.shape, jnp.float32)
         for part, tile in zip(parts, ids):
-            total = total + jnp.where(rows == tile, jnp.exp(part - top), 0.0)
-        return jnp.where(total > 0.0, top + jnp.log(total), negative_floor)
+            total = total + jnp.where(rows == tile, jnp.exp2(part - top), 0.0)
+        return jnp.where(total > 0.0, top + jnp.log2(total), negative_floor)
 
     def merge_sums(parts, ids, rows):
         total = jnp.zeros(rows.shape, jnp.float32)
@@ -147,10 +158,12 @@
     def row_first(k, carry):
         pltpu.make_async_copy(cost_hbm.at[k], cost.at[k], cost_sem.at[k]).wait()
         for c in range(chunks):
-            tile = cost[k, c * ROWS : (c + 1) * ROWS, :].astype(jnp.float32)
+            rows = slice(c * ROWS, (c + 1) * ROWS)
+            tile = cost[k, rows, :].astype(jnp.float32) * inverse_eps
+            q[k, rows, :] = tile
             low = jnp.min(tile, axis=1, keepdims=True)
-            total = jnp.sum(jnp.exp((low - tile) * inverse_eps), axis=1, keepdims=True)
-            put_column(k, c, jnp.log(total) - low * inverse_eps)
+            total = jnp.sum(jnp.exp2(low - tile), axis=1, keepdims=True)
+            put_column(k, c, jnp.log2(total) - low)
         return carry
 
     lax.fori_loop(0, cap, row_first, 0)
@@ -158,21 +171,21 @@
     row_buf1[0] = merge_logs([slot_rows[k : k + 1, :] for k in range(cap)], src_id, src_rows)
     pl.semaphore_wait(barrier, n_tgt - 1 + n_src - 1)
     exchange(row_buf1, "tgt", my_tgt, n_tgt, row_send1, row_recv1)
-    spread_rows(jnp.log(src_mass_ref[...]) - logsumexp0(row_buf1[...]))
+    spread_rows(jnp.log2(src_mass_ref[...]) - logsumexp0(row_buf1[...]))
 
     def col_first(k, carry):
-        s = lax.rem(pairs_ref[k, 0], src_tiles)
+        s = lax.rem(pairs_ref[0, k], src_tiles)
         top = jnp.full((8, edge), negative_floor, jnp.float32)
         for c in range(chunks):
             rows = slice(c * ROWS, (c + 1) * ROWS)
-            score = wide(row_pot[s, rows, :]) - cost[k, rows, :].astype(jnp.float32) * inverse_eps
+            score = wide(row_pot[s, rows, :]) - q[k, rows, :]
             q[k, rows, :] = score
             top = jnp.maximum(top, jnp.max(score.reshape(ROWS // 8, 8, edge), axis=0))
         top = jnp.broadcast_to(jnp.max(top, axis=0, keepdims=True), (8, edge))
         total = jnp.zeros((8, edge), jnp.float32)
         for c in range(chunks):
             rows = slice(c * ROWS, (c + 1) * ROWS)
-            value = jnp.exp(q[k, rows, :].reshape(ROWS // 8, 8, edge) - top[None])
+            value = jnp.exp2(q[k, rows, :].reshape(ROWS // 8, 8, edge) - top[None])
             q[k, rows, :] = value.reshape(ROWS, edge)
             total = total + jnp.sum(value, axis=0)
         col_stab[k] = top
@@ -181,17 +194,17 @@
 
     lax.fori_loop(0, cap, col_first, 0)
     col_buf1[0] = merge_logs(
-        [col_stab[k, 0:1, :] + jnp.log(col_sum[k, 0:1, :]) for k in range(cap)], tgt_id, tgt_rows
+        [col_stab[k, 0:1, :] + jnp.log2(col_sum[k, 0:1, :]) for k in range(cap)], tgt_id, tgt_rows
     )
     exchange(col_buf1, "src", my_src, n_src, col_send1, col_recv1)
-    potential = jnp.log(tgt_mass_ref[...]) - logsumexp0(col_buf1[...])
+    potential = jnp.log2(tgt_mass_ref[...]) - logsumexp0(col_buf1[...])
     for t in range(tgt_tiles):
         tgt_pot[t] = jnp.broadcast_to(potential[t : t + 1, :], (8, edge))
 
     def row_second(k, carry):
-        t = lax.rem(pairs_ref[k, 1], tgt_tiles)
+        t = lax.rem(pairs_ref[1, k], tgt_tiles)
         alive = jnp.full((8, edge), k, jnp.int32) < count
-        factor = jnp.where(alive, jnp.exp(tgt_pot[t] + col_stab[k]), 0.0)
+        factor = jnp.where(alive, jnp.exp2(tgt_pot[t] + col_stab[k]), 0.0)
         col_fac[k] = factor
         for c in range(chunks):
             rows = slice(c * ROWS, (c + 1) * ROWS)
@@ -206,7 +219,7 @@
     spread_rows(src_mass_ref[...] / jnp.sum(row_buf2[...], axis=0))
 
     def col_second(k, carry):
-        s = lax.rem(pairs_ref[k, 0], src_tiles)
+        s = lax.rem(pairs_ref[0, k], src_tiles)
         total = jnp.zeros((8, edge), jnp.float32)
         for c in range(chunks):
             rows = slice(c * ROWS, (c + 1) * ROWS)
@@ -228,8 +241,8 @@
         ).wait()
 
     def map_slot(k, carry):
-        s = lax.rem(pairs_ref[k, 0], src_tiles)
-        t = lax.rem(pairs_ref[k, 1], tgt_tiles)
+        s = lax.rem(pairs_ref[0, k], src_tiles)
+        t = lax.rem(pairs_ref[1, k], tgt_tiles)
         factor = tgt_pot[t] * col_fac[k]
         left = tgts[t]
         for h in range(edge // 256):
@@ -250,33 +263,52 @@
 
     share = out_ref.shape[1]
     tall = dim + PAD
-    low_half = lax.broadcasted_iota(jnp.int32, (tall, LANES), 0) >= dim + PAD // 2
-    for s in range(src_tiles):
-        picks = [jnp.where(src_id[k] == s, 1.0, 0.0) for k in range(cap)]
-        for c in range(edge // LANES):
-            total = jnp.zeros((tall, LANES), jnp.float32)
-            for k in range(cap):
-                total = total + prods[k, :, c * LANES : (c + 1) * LANES] * picks[k]
-            rest = total - total.astype(jnp.bfloat16).astype(jnp.float32)
-            total = jnp.where(low_half, rest, total)
-            place = s * edge + c * LANES
-            start = place % share
-            out_send[place // share, :, start : start + LANES] = total.astype(jnp.bfloat16)
-
+    core, layer, layers = lax.rem(my_tgt, 2), my_tgt // 2, n_tgt // 2
+
+    def pair_copy(j):
+        return pltpu.make_async_remote_copy(
+            src_ref=out_part.at[2 * j + 1 - core],
+            dst_ref=pair_recv.at[j],
+            send_sem=pair_send_sem.at[j],
+            recv_sem=pair_recv_sem.at[j],
+            device_id={"tgt": my_tgt + 1 - 2 * core},
+            device_id_type=MESH,
+        )
+
+    picks = [
+        [jnp.where(src_id[k] == s, 1.0, 0.0) for k in range(cap)] for s in range(src_tiles)
+    ]
+    for place in range(0, src_tiles * edge, LANES):
+        s, start = place // edge, place % edge
+        total = jnp.zeros((tall, LANES), jnp.float32)
+        for k in range(cap):
+            total = total + prods[k, :, start : start + LANES] * picks[s][k]
+        block, start = place // share, place % share
+        out_part[block, :, start : start + LANES] = total
+        if (place + LANES) % (2 * share) == 0:
+            pair_copy(block // 2).start()
+
+    low_half = lax.broadcasted_iota(jnp.int32, (tall, share), 0) >= dim + PAD // 2
     copies = []
-    for off in range(1, n_tgt):
-        peer = lax.rem(my_tgt + off, n_tgt)
+    for off in range(1, layers):
+        other = lax.rem(layer + off, layers)
+        pair_copy(other).wait()
+        total = out_part[2 * other + core] + pair_recv[other]
+        rest = total - total.astype(jnp.bfloat16).astype(jnp.float32)
+        out_send[off - 1] = jnp.where(low_half, rest, total).astype(jnp.bfloat16)
         copy = pltpu.make_async_remote_copy(
-            src_ref=out_send.at[peer],
+            src_ref=out_send.at[off - 1],
             dst_ref=out_recv.at[off - 1],
             send_sem=out_send_sem.at[off - 1],
             recv_sem=out_recv_sem.at[off - 1],
-            device_id={"tgt": peer},
+            device_id={"tgt": 2 * other + core},
             device_id_type=MESH,
         )
         copy.start()
         copies.append(copy)
-    total = out_send[my_tgt].astype(jnp.float32)
+    pair_copy(layer).wait()
+    total = out_part[2 * layer + core] + pair_recv[layer]
+    total = jnp.where(low_half, 0.0, total)
     for off, copy in enumerate(copies):
         copy.wait()
         total = total + out_recv[off].astype(jnp.float32)
@@ -313,12 +345,16 @@
             pltpu.VMEM((cap, 8, edge), f32),
             pltpu.VMEM((cap, 8, edge), f32),
             pltpu.VMEM((tgt_tiles, 8, edge), f32),
+            pltpu.VMEM((src_tiles, edge), f32),
+            pltpu.VMEM((tgt_tiles, edge), f32),
             pltpu.VMEM((n_tgt, src_tiles, edge), f32),
             pltpu.VMEM((n_tgt, src_tiles, edge), f32),
             pltpu.VMEM((n_src, tgt_tiles, edge), f32),
             pltpu.VMEM((n_src, tgt_tiles, edge), f32),
-            pltpu.VMEM((n_tgt, tall, share), bf16),
-            pltpu.VMEM((n_tgt - 1, tall, share), bf16),
+            pltpu.VMEM((n_tgt, tall, share), f32),
+            pltpu.VMEM((n_tgt // 2, tall, share), f32),
+            pltpu.VMEM((n_tgt // 2 - 1, tall, share), bf16),
+            pltpu.VMEM((n_tgt // 2 - 1, tall, share), bf16),
             dma((cap,)),
             dma((tgt_tiles,)),
             dma((n_tgt - 1,)),
@@ -329,18 +365,20 @@
             dma((n_src - 1,)),
             dma((n_src - 1,)),
             dma((n_src - 1,)),
-            dma((n_tgt - 1,)),
-            dma((n_tgt - 1,)),
+            dma((n_tgt // 2,)),
+            dma((n_tgt // 2,)),
+            dma((n_tgt // 2 - 1,)),
+            dma((n_tgt // 2 - 1,)),
         ],
         compiler_params=pltpu.CompilerParams(
             collective_id=0, has_side_effects=True, vmem_limit_bytes=56 * 1024 * 1024
         ),
     )(
-        tile_pairs,
+        tile_pairs.T,
         tile_counts,
         tile_cost,
-        src_mass.reshape(src_tiles, edge),
-        tgt_mass.reshape(tgt_tiles, edge),
+        src_mass,
+        tgt_mass,
         targets_t,
     )
 

time: 56.3 us -> 49.1 us (0.87); the launches traced: 55.3 us -> 48.8 us
  local copies, waits for them, and re-layouts: 5.56 us -> 1.54 us
  Pallas kernels: 49 us -> 46.6 us
    reshape x2 -> x0, local copies, waits for them, and re-layouts: 2.66 us -> none  [the longest x1 1.35 us: local(): tgt_mass.reshape(tgt_tiles, edge)]
    pallas_call x1, Pallas kernels: 49 us -> 46.6 us  [local(): pl.pallas_call(functools.partial(kernel, n_src, n_tgt), out_shape=jax.Sha...]
    unnamed x2 -> x1, local copies, waits for them, and re-layouts: 2.9 us -> 1.54 us
where the time goes in v2:
time: 49.1 us; the launch traced here: 48.8 us
  Pallas kernels  46.6 us (95%)
  local copies, waits for them, and re-layouts  1.54 us (3%)
  between operations  0.66 us (1%)
    pallas_call x1, Pallas kernels, local(): pl.pallas_call(functools.partial(kernel, n_src, n_tgt), out_shape=jax.Sha...  46.6 us
    unnamed x1, local copies, waits for them, and re-layouts  1.54 us

profile of v2, /device:TPU:0, one launch (start us, length us, event | category | flops | bytes accessed | tf_op | source)
XLA Modules:
  0.0 48.8 jit_solution(4204083719567061684)
XLA Ops:
  0.7 46.6 %shard_map.64 = f32[64,384]{1,0:T(8,128)} custom-call(s32[2,12]{1,0:T(2,128)} %bitcast.1, s32[1]{0:T(128)S(6)} %copy.8.count_ref, bf16[12,512,512]{2,1,0:T(8,128)(2,1)} %cost_hbm.1, f32[3072]{0:T(1024)} %src_mass_flat.1, f32[6144]{0:T(1024)} %tgt_mass_flat.1, bf16[64,6144]{1,0:T(8,128)(2,1)} %targets_hbm.1), custom_call_target="tpu_custom_call" | custom-call | tf_op jit(solution)/shard_map/pallas_call | solution.py:330
  47.3 1.5 %copy.9 = f32[64,384]{1,0:T(8,128)} copy(f32[64,384]{1,0:T(8,128)} %shard_map.64) | data formatting | bytes 196608

commit v3 on v2

--- a/solution.py
+++ b/solution.py
@@ -32,6 +32,7 @@
     out_ref,
     cost,
     q,
+    low,
     tgts,
     prods,
     slot_cols,
@@ -155,44 +156,70 @@
             total = total + jnp.where(rows == tile, part, 0.0)
         return total
 
-    def row_first(k, carry):
-        pltpu.make_async_copy(cost_hbm.at[k], cost.at[k], cost_sem.at[k]).wait()
-        for c in range(chunks):
-            rows = slice(c * ROWS, (c + 1) * ROWS)
-            tile = cost[k, rows, :].astype(jnp.float32) * inverse_eps
-            q[k, rows, :] = tile
-            low = jnp.min(tile, axis=1, keepdims=True)
-            total = jnp.sum(jnp.exp2(low - tile), axis=1, keepdims=True)
-            put_column(k, c, jnp.log2(total) - low)
+    def halves(combine, block):
+        parts = [block[:, at : at + LANES] for at in range(0, edge, LANES)]
+        return functools.reduce(combine, parts)
+
+    def in_pairs(step):
+        def both(i, carry):
+            step(2 * i)
+            step(2 * i + 1)
+            return carry
+
+        lax.fori_loop(0, cap // 2, both, 0)
+
+    def row_first(i, carry):
+        for u in range(2):
+            k = 2 * i + u
+            pltpu.make_async_copy(cost_hbm.at[k], cost.at[k], cost_sem.at[k]).wait()
+            for c in range(chunks):
+                rows = slice(c * ROWS, (c + 1) * ROWS)
+                tile = cost[k, rows, :].astype(jnp.float32) * inverse_eps
+                q[k, rows, :] = tile
+                least = jnp.min(halves(jnp.minimum, tile), axis=1, keepdims=True)
+                low[u, rows, :] = jnp.broadcast_to(least, (ROWS, LANES))
+        for u in range(2):
+            k = 2 * i + u
+            for c in range(chunks):
+                rows = slice(c * ROWS, (c + 1) * ROWS)
+                value = jnp.exp2(wide(low[u, rows, :]) - q[k, rows, :])
+                total = jnp.sum(halves(jnp.add, value), axis=1, keepdims=True)
+                put_column(k, c, jnp.log2(total) - low[u, rows, :])
         return carry
 
-    lax.fori_loop(0, cap, row_first, 0)
+    lax.fori_loop(0, cap // 2, row_first, 0)
     slots_as_rows()
     row_buf1[0] = merge_logs([slot_rows[k : k + 1, :] for k in range(cap)], src_id, src_rows)
     pl.semaphore_wait(barrier, n_tgt - 1 + n_src - 1)
     exchange(row_buf1, "tgt", my_tgt, n_tgt, row_send1, row_recv1)
     spread_rows(jnp.log2(src_mass_ref[...]) - logsumexp0(row_buf1[...]))
 
-    def col_first(k, carry):
-        s = lax.rem(pairs_ref[0, k], src_tiles)
-        top = jnp.full((8, edge), negative_floor, jnp.float32)
-        for c in range(chunks):
-            rows = slice(c * ROWS, (c + 1) * ROWS)
-            score = wide(row_pot[s, rows, :]) - q[k, rows, :]
-            q[k, rows, :] = score
-            top = jnp.maximum(top, jnp.max(score.reshape(ROWS // 8, 8, edge), axis=0))
-        top = jnp.broadcast_to(jnp.max(top, axis=0, keepdims=True), (8, edge))
-        total = jnp.zeros((8, edge), jnp.float32)
-        for c in range(chunks):
-            rows = slice(c * ROWS, (c + 1) * ROWS)
-            value = jnp.exp2(q[k, rows, :].reshape(ROWS // 8, 8, edge) - top[None])
-            q[k, rows, :] = value.reshape(ROWS, edge)
-            total = total + jnp.sum(value, axis=0)
-        col_stab[k] = top
-        col_sum[k] = jnp.broadcast_to(jnp.sum(total, axis=0, keepdims=True), (8, edge))
+    def col_first(i, carry):
+        tops = []
+        for u in range(2):
+            k = 2 * i + u
+            s = lax.rem(pairs_ref[0, k], src_tiles)
+            top = jnp.full((8, edge), negative_floor, jnp.float32)
+            for c in range(chunks):
+                rows = slice(c * ROWS, (c + 1) * ROWS)
+                score = wide(row_pot[s, rows, :]) - q[k, rows, :]
+                top = jnp.maximum(top, jnp.max(score.reshape(ROWS // 8, 8, edge), axis=0))
+            tops.append(jnp.broadcast_to(jnp.max(top, axis=0, keepdims=True), (8, edge)))
+        for u in range(2):
+            k = 2 * i + u
+            s = lax.rem(pairs_ref[0, k], src_tiles)
+            total = jnp.zeros((8, edge), jnp.float32)
+            for c in range(chunks):
+                rows = slice(c * ROWS, (c + 1) * ROWS)
+                score = (wide(row_pot[s, rows, :]) - q[k, rows, :]).reshape(ROWS // 8, 8, edge)
+                value = jnp.exp2(score - tops[u][None])
+                q[k, rows, :] = value.reshape(ROWS, edge)
+                total = total + jnp.sum(value, axis=0)
+            col_stab[k] = tops[u]
+            col_sum[k] = jnp.broadcast_to(jnp.sum(total, axis=0, keepdims=True), (8, edge))
         return carry
 
-    lax.fori_loop(0, cap, col_first, 0)
+    lax.fori_loop(0, cap // 2, col_first, 0)
     col_buf1[0] = merge_logs(
         [col_stab[k, 0:1, :] + jnp.log2(col_sum[k, 0:1, :]) for k in range(cap)], tgt_id, tgt_rows
     )
@@ -201,7 +228,7 @@
     for t in range(tgt_tiles):
         tgt_pot[t] = jnp.broadcast_to(potential[t : t + 1, :], (8, edge))
 
-    def row_second(k, carry):
+    def row_second(k):
         t = lax.rem(pairs_ref[1, k], tgt_tiles)
         alive = jnp.full((8, edge), k, jnp.int32) < count
         factor = jnp.where(alive, jnp.exp2(tgt_pot[t] + col_stab[k]), 0.0)
@@ -209,16 +236,16 @@
         for c in range(chunks):
             rows = slice(c * ROWS, (c + 1) * ROWS)
             value = q[k, rows, :].reshape(ROWS // 8, 8, edge) * factor[None]
-            put_column(k, c, jnp.sum(value.reshape(ROWS, edge), axis=1, keepdims=True))
-        return carry
-
-    lax.fori_loop(0, cap, row_second, 0)
+            total = halves(jnp.add, value.reshape(ROWS, edge))
+            put_column(k, c, jnp.sum(total, axis=1, keepdims=True))
+
+    in_pairs(row_second)
     slots_as_rows()
     row_buf2[0] = merge_sums([slot_rows[k : k + 1, :] for k in range(cap)], src_id, src_rows)
     exchange(row_buf2, "tgt", my_tgt, n_tgt, row_send2, row_recv2)
     spread_rows(src_mass_ref[...] / jnp.sum(row_buf2[...], axis=0))
 
-    def col_second(k, carry):
+    def col_second(k):
         s = lax.rem(pairs_ref[0, k], src_tiles)
         total = jnp.zeros((8, edge), jnp.float32)
         for c in range(chunks):
@@ -226,9 +253,8 @@
             value = q[k, rows, :] * wide(row_pot[s, rows, :])
             total = total + jnp.sum(value.reshape(ROWS // 8, 8, edge), axis=0)
         col_sum[k] = jnp.broadcast_to(jnp.sum(total, axis=0, keepdims=True), (8, edge)) * col_fac[k]
-        return carry
-
-    lax.fori_loop(0, cap, col_second, 0)
+
+    in_pairs(col_second)
     col_buf2[0] = merge_sums([col_sum[k, 0:1, :] for k in range(cap)], tgt_id, tgt_rows)
     exchange(col_buf2, "src", my_src, n_src, col_send2, col_recv2)
     potential = tgt_mass_ref[...] / jnp.sum(col_buf2[...], axis=0)
@@ -240,7 +266,7 @@
             targets_hbm.at[:, pl.ds(t * edge, edge)], tgts.at[t, pl.ds(0, dim)], tgts_sem.at[t]
         ).wait()
 
-    def map_slot(k, carry):
+    def map_slot(k):
         s = lax.rem(pairs_ref[0, k], src_tiles)
         t = lax.rem(pairs_ref[1, k], tgt_tiles)
         factor = tgt_pot[t] * col_fac[k]
@@ -257,9 +283,8 @@
                 (((1,), (1,)), ((), ())),
                 preferred_element_type=jnp.float32,
             )
-        return carry
-
-    lax.fori_loop(0, cap, map_slot, 0)
+
+    in_pairs(map_slot)
 
     share = out_ref.shape[1]
     tall = dim + PAD
@@ -335,6 +360,7 @@
         scratch_shapes=[
             pltpu.VMEM((cap, edge, edge), bf16),
             pltpu.VMEM((cap, edge, edge), f32),
+            pltpu.VMEM((2, edge, LANES), f32),
             pltpu.VMEM((tgt_tiles, tall, edge), bf16),
             pltpu.VMEM((cap, tall, edge), f32),
             pltpu.VMEM((edge, LANES), f32),

time: 49.1 us -> 47.9 us (0.976)
  Pallas kernels: 46.6 us -> 45.5 us
    pallas_call x1, Pallas kernels: 46.6 us -> 45.5 us  [local(): pl.pallas_call(functools.partial(kernel, n_src, n_tgt), out_shape=jax.Sha...]
where the time goes in v3:
time: 47.9 us; the launch traced here: 47.7 us
  Pallas kernels  45.5 us (95%)
  local copies, waits for them, and re-layouts  1.54 us (3%)
  between operations  0.66 us (1%)
    pallas_call x1, Pallas kernels, local(): pl.pallas_call(functools.partial(kernel, n_src, n_tgt), out_shape=jax.Sha...  45.5 us
    unnamed x1, local copies, waits for them, and re-layouts  1.54 us

profile of v3, /device:TPU:0, one launch (start us, length us, event | category | flops | bytes accessed | tf_op | source)
XLA Modules:
  0.0 47.7 jit_solution(7267466451668884676)
XLA Ops:
  0.7 45.5 %shard_map.64 = f32[64,384]{1,0:T(8,128)} custom-call(s32[2,12]{1,0:T(2,128)} %bitcast.1, s32[1]{0:T(128)S(6)} %copy.8.count_ref, bf16[12,512,512]{2,1,0:T(8,128)(2,1)} %cost_hbm.1, f32[3072]{0:T(1024)} %src_mass_flat.1, f32[6144]{0:T(1024)} %tgt_mass_flat.1, bf16[64,6144]{1,0:T(8,128)(2,1)} %targets_hbm.1), custom_call_target="tpu_custom_call" | custom-call | tf_op jit(solution)/shard_map/pallas_call | solution.py:355
  46.1 1.5 %copy.9 = f32[64,384]{1,0:T(8,128)} copy(f32[64,384]{1,0:T(8,128)} %shard_map.64) | data formatting | bytes 196608
